TPU v7x, 32 devices: a whole 2x2x4 slice. The times are simulated.
32 devices in a mesh: grid: 4 (over z), rep: 8 (over y, x, core).
Axes of the slice: x: 2, y: 2, z: 4, core: 2. Of those that a mesh axis runs over, the one named last changes fastest.
Arguments:
- amplitudes: bfloat16 [96, 960, 960], P('grid', 'rep'), may hold values from -6 to 6
- vvvv_panel: bfloat16 [960, 960, 1920], P('rep', 'grid'), may hold values from -0.01171875 to 0.01171875
- fock_window: bfloat16 [960, 2], P('rep'), may hold values from -0.375 to 0.375
- orbital_irrep: int32 [960], replicated, may hold values from 0 to 3, as said below
- pair_irrep: int32 [96], replicated, may hold values from 0 to 3
- virtual_panel: int32 [2], replicated, may hold values from 0 to 959
Outputs:
- residual: float32 [96, 2, 960], P('rep', None, 'grid')
Inputs may be any that keep to these rules, and one draw needn't show every extreme that they name: `orbital_irrep`: the virtual orbitals form four contiguous runs of 240 orbitals each; every orbital of a run has the same irrep, and each irrep 0 to 3 holds exactly one run, in an order that varies from draw to draw.
All inputs are finite; a program needn't handle non-finite values.
Results may differ from a plain program's by a relative error of at most 0.00035.
Values may be sent and summed in bfloat16 or wider, within the bound.
A program may use at most 384 MiB of HBM per device.

v0:
```python
import jax
import jax.numpy as jnp
from jax import lax
from jax.sharding import PartitionSpec as P


def shards(amplitudes, vvvv_panel, fock_window, orbital_irrep, pair_irrep, virtual_panel):
    pair_local = amplitudes.shape[0]
    virt_local = amplitudes.shape[1]
    full_virt = amplitudes.shape[2]
    col_local = vvvv_panel.shape[1]
    panel_width = vvvv_panel.shape[2] // full_virt
    grid_index = lax.axis_index("grid")
    rep_index = lax.axis_index("rep")
    row_irreps = lax.dynamic_slice_in_dim(orbital_irrep, rep_index * virt_local, virt_local, 0)
    col_irreps = lax.dynamic_slice_in_dim(orbital_irrep, grid_index * col_local, col_local, 0)
    pair_local_irreps = lax.dynamic_slice_in_dim(pair_irrep, grid_index * pair_local, pair_local, 0)
    panel_irrep = orbital_irrep[virtual_panel]
    row_sym = jnp.bitwise_xor(row_irreps[:, None], orbital_irrep[None, :])
    amp_mask = row_sym[None, :, :] == pair_local_irreps[:, None, None]
    masked_amps = jnp.where(amp_mask, amplitudes, jnp.zeros_like(amplitudes))
    target_cols = jnp.bitwise_xor(col_irreps[:, None], panel_irrep[None, :])
    panel_four = vvvv_panel.reshape(virt_local, col_local, panel_width, full_virt)
    w_mask = row_sym[:, None, None, :] == target_cols[None, :, :, None]
    masked_w = jnp.where(w_mask, panel_four, jnp.zeros_like(panel_four))
    fock_mask = row_irreps[:, None] == panel_irrep[None, :]
    masked_f = jnp.where(fock_mask, fock_window, jnp.zeros_like(fock_window))
    col_start = grid_index * col_local
    block_rows = lax.all_gather(masked_amps, "grid", axis=0, tiled=True)
    row_count = block_rows.shape[0]
    ladder = jnp.einsum("ncd,cabd->nba", block_rows, masked_w, preferred_element_type=jnp.float32)
    own_cols = lax.dynamic_slice_in_dim(block_rows, col_start, col_local, 2)
    fock_term = jnp.einsum("pca,cb->pba", own_cols, masked_f, preferred_element_type=jnp.float32)
    partials = (ladder + fock_term).reshape(row_count, panel_width * col_local)
    pair_total = partials.shape[0]
    out_rows = pair_total // lax.axis_size("rep")
    summed = lax.psum_scatter(partials, "rep", scatter_dimension=0, tiled=True)
    return summed.reshape(out_rows, panel_width, col_local)


def solution(mesh):
    return jax.shard_map(
        shards,
        mesh=mesh,
        in_specs=(P("grid", "rep", None), P("rep", "grid", None), P("rep", None), P(), P(), P()),
        out_specs=P("rep", None, "grid"),
        check_vma=False,
    )
```

profile of v0, /device:TPU:1, one launch (start us, length us, event | category | flops | bytes accessed | tf_op | source)
XLA Modules:
  0.0 514.5 jit_solution(10889192295374273812)
XLA Ops:
  6.5 0.0 all-gather.2.cloned.1.call-start
  6.5 0.8 dynamic_slice.12
  7.3 0.8 broadcast_xor_fusion
  8.1 0.7 dynamic_slice.14
  8.8 9.2 %compare_select_fusion.2 = bf16[24,120,960]{2,0,1:T(8,128)(2,1)} fusion(bf16[24,120,960]{2,1,0:T(8,128)(2,1)} %param.6, s32[120,960]{1,0:T(8,128)S(1)} %broadcast_xor_fusion, s32[24]{0:T(128)S(1)} %dynamic_slice.14), kind=kLoop, calls=%fused_computation.8 | loop fusion | flops 5529600 | bytes 11520096 | tf_op jit(solution)/shard_map/jit(_where)/select_n | solution.py:21
  18.1 0.0 all-gather.2.cloned.1.call-update
  18.1 0.7 compare_select_fusion.7
  18.8 1.3 gather_fusion
  20.1 0.8 dynamic_slice.13
  20.9 0.0 copy-start.1
  20.9 278.2 %reshape.85 = bf16[120,240,2,960]{3,2,1,0:T(2,128)(2,1)} reshape(bf16[120,240,1920]{2,1,0:T(8,128)(2,1)} %param.7) | data formatting | bytes 221184000 | tf_op jit(solution)/shard_map/reshape | solution.py:23
  299.0 0.1 broadcast_xor_fusion.1
  299.1 121.1 %all-gather.2.cloned.1.call-done = bf16[96,120,960]{2,0,1:T(8,128)(2,1)} async-done(((bf16[24,120,960]{2,0,1:T(8,128)(2,1)}), bf16[96,120,960]{2,0,1:T(8,128)(2,1)}) %all-gather.2.cloned.1.call-update) | async-done | bytes 22118416 | tf_op jit(solution)/shard_map/all_gather | solution.py:29
  420.2 6.7 %constant_dynamic-slice_fusion.1 = bf16[96,120,240]{2,0,1:T(8,128)(2,1)S(1)} fusion(bf16[96,120,960]{2,0,1:T(8,128)(2,1)} %all-gather.2.cloned.1.call-done, s32[]{:T(128)S(6)} %select_n.26), kind=kLoop, calls=%fused_computation.23 | loop fusion | bytes 11059204 | tf_op jit(solution)/shard_map/dynamic_slice | solution.py:32
  426.9 0.0 copy-done.1
  426.9 3.4 fusion.7
  430.3 0.0 copy-start
  430.3 53.1 %fusion.12 = f32[96,2,240]{2,0,1:T(8,128)S(1)} fusion(bf16[96,120,960]{2,0,1:T(8,128)(2,1)} %all-gather.2.cloned.1.call-done, bf16[120,240,2,960]{3,2,1,0:T(2,128)(2,1)} %reshape.85, s32[240,2]{0,1:T(2,128)S(1)} %broadcast_xor_fusion.1, s32[120,960]{1,0:T(8,128)S(1)} %broadcast_xor_fusion, f32[2,96,240]{2,0,1:T(2,128)S(1)} %fusion.7), kind=kOutput, calls=%fused_computation.12 | convolution fusion | flops 10727470080 | bytes 133541760 | tf_op jit(solution)/shard_map/ncd,cabd->nba/dot_general | solution.py:31
  483.4 0.2 copy.20
  483.5 0.2 reshape.86
  483.7 14.7 %fusion = f32[16,480]{1,0:T(8,128)S(1)} fusion(f32[96,480]{1,0:T(8,128)S(1)} %reshape.86), kind=kCustom, calls=%all-reduce-scatter | all-reduce-scatter fusion | flops 61441 | bytes 215552
  498.4 2.0 collective-permute-start
  500.4 4.9 collective-permute-start.1
  505.4 0.0 copy-done
  505.4 0.6 dynamic-slice.4
  506.6 0.0 collective-permute-done.1
  506.7 0.0 collective-permute-done
  506.7 0.3 concatenate
  507.0 0.7 reshape.87
  (3 shorter events, 0.0 us)
Async XLA Ops:
  6.5 413.7 %all-gather.2.cloned.1.call-start = ((), (), s32[]{:S(2)}) async-start(), calls=%async_computation | async-start | bytes 29491200 | tf_op jit(solution)/shard_map/all_gather | solution.py:29
  20.9 406.0 %copy-start.1 = (bf16[120,2]{0,1:T(2,128)(2,1)S(1)}, bf16[120,2]{0,1:T(2,128)(2,1)}, u32[]{:S(2)}) copy-start(bf16[120,2]{0,1:T(2,128)(2,1)} %param.8) | copy-start | bytes 1444
  430.3 75.1 %copy-start = (u32[32]{0:T(128)S(1)}, u32[32]{0:T(128)}, u32[]{:S(2)}) copy-start(u32[32]{0:T(128)} %constant.28) | copy-start | bytes 388
  498.4 8.3 %collective-permute-start = (f32[16,480]{1,0:T(8,128)S(1)}, f32[16,480]{1,0:T(8,128)S(1)}, u32[]{:S(2)}, u32[]{:S(2)}) collective-permute-start(f32[16,480]{1,0:T(8,128)S(1)} %fusion), channel_id=1, source_target_pairs={{0,1},{1,2},{2,3},{3,4},{4,5},{5,6},{6,7},{8,9},{9,10},{10,11},{11... | collective-permute-start | bytes 92168
  500.4 6.2 %collective-permute-start.1 = (f32[12,480]{1,0:T(8,128)S(1)}, f32[12,480]{1,0:T(8,128)S(1)}, u32[]{:S(2)}, u32[]{:S(2)}) collective-permute-start(f32[12,480]{1,0:T(8,128)S(1)} %slice.2), channel_id=1, source_target_pairs={{0,2},{1,3},{2,4},{3,5},{4,6},{5,7},{8,10},{9,11},{10,12},{11,13},... | collective-permute-start | bytes 69128
Sparse Core Ops, SparseCore 0:
  18.2 401.9 all-gather.1
where the time goes:
time: 518 us; the launch traced here: 515 us
  local copies, waits for them, and re-layouts  290 us (56%)
  waiting for transfers between devices  121 us (23%)
  matrix products  56.5 us (11%)
  blocking collectives  14.7 us (3%)
  between operations  14.2 us (3%)
  other arithmetic  10.8 us (2%)
  starting transfers between devices  6.98 us (1%)
    reshape x1, local copies, waits for them, and re-layouts, shards(): vvvv_panel.reshape(virt_local, col_local, panel_width, full_virt)  278 us
    all_gather x1, waiting for transfers between devices, shards(): block_rows = lax.all_gather(masked_amps, 'grid', axis=0, tiled=True)  121 us
    dot_general x1, matrix products, shards(): jnp.einsum('ncd,cabd->nba', block_rows, masked_w, preferred_element_type=...  53.1 us
    unnamed x1, blocking collectives  14.7 us
  transfers between devices with their start and end apart: 3, of which 1 were waited for; matrix products, arithmetic and copies ran while one was open for 55% of the time, Pallas kernels for 0%

commit v1 on v0

v1 whole, which is shorter than its diff:
```python
import functools

import jax
import jax.numpy as jnp
from jax import lax
from jax.experimental import pallas as pl
from jax.experimental.pallas import tpu as pltpu
from jax.sharding import PartitionSpec as P

LANES = 128
SPAN = 256
CHUNKS = 3


def ladder_kernel(steps, panel, scalars, fock, amps, *refs):
    tiles = refs[: 3 * panel]
    out = refs[3 * panel]
    acc, facc, wide, turned = refs[3 * panel + 1 :]
    step = pl.program_id(0)
    depth, cols, _ = tiles[0].shape

    @pl.when(step == 0)
    def _():
        acc[...] = jnp.zeros_like(acc)
        facc[...] = jnp.zeros_like(facc)

    lane = lax.broadcasted_iota(jnp.int32, (cols, LANES), 1)
    for c in range(depth):
        at = slice(c * SPAN, (c + 1) * SPAN)
        part = amps[:, at].astype(jnp.float32)
        for b in range(panel):
            facc[b] += fock[(step * depth + c) * panel + b] * part
            turned[b, :, at] = pltpu.roll(part, scalars[panel + b], 1).astype(jnp.bfloat16)
            first, second, third = tiles[3 * b : 3 * b + 3]
            low = jnp.where(lane >= scalars[2 * panel + b], first[c], third[c])
            wide[b, :, c * SPAN : c * SPAN + LANES] = low
            wide[b, :, c * SPAN + LANES : (c + 1) * SPAN] = second[c]
    for b in range(panel):
        acc[b] += lax.dot_general(turned[b], wide[b], (((1,), (1,)), ((), ())), preferred_element_type=jnp.float32)

    @pl.when(step == steps - 1)
    def _():
        for b in range(panel):
            own = pltpu.roll(facc[b], scalars[3 * panel], 1)
            out[b] = acc[b] + own[:, :cols]


def ladder(scalars, fock, amps, w, first_row, rows, full_virt):
    panel = w.shape[2] // full_virt
    cols = w.shape[1]
    pairs = amps.shape[0]
    depth = max(d for d in range(1, 9) if rows % d == 0)
    steps = rows // depth
    last_tile = w.shape[2] // LANES - 1
    offset = first_row // depth

    def tile_map(b, j):
        def index(i, scalars, fock):
            return (i + offset, 0, jnp.minimum(scalars[b] + j, last_tile))

        return index

    w_specs = [pl.BlockSpec((depth, cols, LANES), tile_map(b, j)) for b in range(panel) for j in range(3)]
    return pl.pallas_call(
        functools.partial(ladder_kernel, steps, panel),
        out_shape=jax.ShapeDtypeStruct((panel, pairs, cols), jnp.float32),
        grid_spec=pltpu.PrefetchScalarGridSpec(
            num_scalar_prefetch=2,
            grid=(steps,),
            in_specs=[pl.BlockSpec((pairs, depth * SPAN), lambda i, s, f: (0, i))] + w_specs,
            out_specs=pl.BlockSpec((panel, pairs, cols), lambda i, s, f: (0, 0, 0)),
            scratch_shapes=[
                pltpu.VMEM((panel, pairs, cols), jnp.float32),
                pltpu.VMEM((panel, pairs, SPAN), jnp.float32),
                pltpu.VMEM((panel, cols, depth * SPAN), jnp.bfloat16),
                pltpu.VMEM((panel, pairs, depth * SPAN), jnp.bfloat16),
            ],
        ),
        compiler_params=pltpu.CompilerParams(vmem_limit_bytes=40 * 1024 * 1024),
        cost_estimate=pl.CostEstimate(
            flops=2 * pairs * rows * SPAN * cols * panel,
            bytes_accessed=rows * cols * 3 * LANES * panel * 2 + pairs * rows * SPAN * 2,
            transcendentals=0,
        ),
    )(scalars, fock, amps, *([w] * (3 * panel)))


def shards(amplitudes, vvvv_panel, fock_window, orbital_irrep, pair_irrep, virtual_panel):
    pair_local, virt_local, full_virt = amplitudes.shape
    col_local = vvvv_panel.shape[1]
    panel = vvvv_panel.shape[2] // full_virt
    run = full_virt // 4
    grid_index = lax.axis_index("grid")
    rep_index = lax.axis_index("rep")
    col_start = grid_index * col_local

    run_irreps = orbital_irrep[::run]
    places = jnp.sum(jnp.where(run_irreps[None, :] == jnp.arange(4)[:, None], jnp.arange(4)[None, :], 0), axis=1).astype(jnp.int32)
    c_irrep = run_irreps[rep_index * virt_local // run]
    a_irrep = run_irreps[col_start // run]
    panel_irrep = orbital_irrep[virtual_panel]

    own_pairs = lax.dynamic_slice_in_dim(pair_irrep, grid_index * pair_local, pair_local, 0)
    pair_run = places[own_pairs ^ c_irrep]
    span_count = -(-full_virt // SPAN)
    compact = jnp.zeros((pair_local, virt_local, SPAN), amplitudes.dtype)
    for q in range(span_count):
        width = min(SPAN, full_virt - q * SPAN)
        piece = amplitudes[:, :, q * SPAN : q * SPAN + width]
        piece = jnp.pad(piece, ((0, 0), (0, 0), (0, SPAN - width)))
        lane_run = (q * SPAN + jnp.arange(SPAN, dtype=jnp.int32)) // run
        compact = jnp.where(lane_run[None, None, :] == pair_run[:, None, None], piece, compact)

    panel_run = places[c_irrep ^ a_irrep ^ panel_irrep]
    starts = jnp.arange(panel, dtype=jnp.int32) * full_virt
    first = starts + panel_run * run
    first_tile = first // LANES
    shift = (starts - first_tile * LANES) % SPAN
    skip = first - first_tile * LANES
    own_shift = (-col_start) % SPAN
    scalars = jnp.concatenate([first_tile, shift, skip, own_shift[None]]).astype(jnp.int32)
    masked_f = jnp.where(panel_irrep[None, :] == c_irrep, fock_window, jnp.zeros_like(fock_window)).astype(jnp.float32)

    chunks = CHUNKS if virt_local % CHUNKS == 0 else 1
    rows = virt_local // chunks
    total = None
    for k in range(chunks):
        part = compact[:, k * rows : (k + 1) * rows, :].reshape(pair_local, rows * SPAN)
        gathered = lax.all_gather(part, "grid", axis=0, tiled=True)
        fock = masked_f[k * rows : (k + 1) * rows].reshape(-1)
        term = ladder(scalars, fock, gathered, vvvv_panel, k * rows, rows, full_virt)
        total = term if total is None else total + term

    pair_count = total.shape[1]
    keep = pair_irrep[None, :] == (panel_irrep ^ a_irrep)[:, None]
    partials = jnp.where(keep[:, :, None], total, 0.0)
    partials = jnp.swapaxes(partials, 0, 1).reshape(pair_count, panel * col_local)
    summed = lax.psum_scatter(partials, "rep", scatter_dimension=0, tiled=True)
    return summed.reshape(pair_count // lax.axis_size("rep"), panel, col_local)


def solution(mesh):
    return jax.shard_map(
        shards,
        mesh=mesh,
        in_specs=(P("grid", "rep", None), P("rep", "grid", None), P("rep", None), P(), P(), P()),
        out_specs=P("rep", None, "grid"),
        check_vma=False,
    )
```

time: 518 us -> 194 us (0.37)
  local copies, waits for them, and re-layouts: 290 us -> 13.4 us
  matrix products: 56.5 us -> 0 us
  Pallas kernels: 0 us -> 28.8 us
  waiting for transfers between devices: 121 us -> 104 us
    reshape x3 -> x5, local copies, waits for them, and re-layouts: 279 us -> 1.22 us  [the longest x1 0.69 us: shards(): return summed.reshape(pair_count // lax.axis_size('rep'), panel, col_local)]
    dot_general x2 -> x0, matrix products: 56.5 us -> none  [the longest x1 53.1 us: shards(): jnp.einsum('ncd,cabd->nba', block_rows, masked_w, preferred_element_type=...]
    pallas_call x0 -> x3, Pallas kernels: none -> 28.8 us  [ladder(): pl.pallas_call(functools.partial(ladder_kernel, steps, panel), out_shape=...]
    all_gather x1 -> x3, waiting for transfers between devices: 121 us -> 104 us  [shards(): gathered = lax.all_gather(part, 'grid', axis=0, tiled=True)]
    dynamic_slice x4 -> x1, local copies, waits for them, and re-layouts: 8.95 us -> 0.65 us  [shards(): a_irrep = run_irreps[col_start // run]]
    unnamed x8 -> x25, local copies, waits for them, and re-layouts: 0.88 us -> 8.21 us
  transfers between devices with their start and end apart: 3 -> 5, of which waited for: 1 -> 3; matrix products, arithmetic and copies ran while one was open for 55% -> 3% of each run, Pallas kernels for 0% -> 10%
where the time goes in v1:
time: 194 us; the launch traced here: 193 us
  waiting for transfers between devices  104 us (54%)
  Pallas kernels  28.8 us (15%)
  between operations  15.3 us (8%)
  blocking collectives  15.1 us (8%)
  local copies, waits for them, and re-layouts  13.4 us (7%)
  other arithmetic  9.86 us (5%)
  starting transfers between devices  6.78 us (3%)
    all_gather x3, waiting for transfers between devices, shards(): gathered = lax.all_gather(part, 'grid', axis=0, tiled=True)  104 us
    pallas_call x3, Pallas kernels, ladder(): pl.pallas_call(functools.partial(ladder_kernel, steps, panel), out_shape=...  28.8 us
    unnamed x1, blocking collectives  15.1 us
    unnamed x25, local copies, waits for them, and re-layouts  8.21 us
    unnamed x2, starting transfers between devices  6.7 us
    select_n x1, other arithmetic, shards(): jnp.where(lane_run[None, None, :] == pair_run[:, None, None], piece, comp...  4.19 us
  transfers between devices with their start and end apart: 5, of which 3 were waited for; matrix products, arithmetic and copies ran while one was open for 3% of the time, Pallas kernels for 10%

profile of v1, /device:TPU:1, one launch (start us, length us, event | category | flops | bytes accessed | tf_op | source)
XLA Modules:
  0.0 193.3 jit_solution(17305570692973436754)
XLA Ops:
  6.6 0.8 slice.33
  7.3 0.1 select_reduce_fusion
  7.4 0.7 fusion.6
  8.1 0.6 fusion.7
  8.8 3.3 %compare_select_fusion.5 = s32[24]{0:T(128)S(1)} fusion(s32[96]{0:T(128)S(1)} %copy-done.6, s32[]{:T(128)S(6)} %select_n.117, s32[]{:T(128)} %bitcast.5, s32[]{:T(128)} %bitcast.6, s32[]{:T(128)} %bitcast.7, s32[]{:T(128)} %bitcast.8, s32[]{:T(128)} %bitcast.1), kind=kLoop, calls=%fused_computation.21 | loop fusion | flops 240 | bytes 216 | tf_op jit(solution)/shard_map/gather | solution.py:104
  12.1 0.1 broadcast_compare_fusion.3
  12.2 4.2 %select_select_fusion = bf16[24,120,256]{2,1,0:T(8,128)(2,1)S(1)} fusion(bf16[24,120,960]{2,1,0:T(8,128)(2,1)} %param.6, bf16[24,120,192]{2,1,0:T(8,128)(2,1)S(1)} %slice-done, pred[24,256]{1,0:T(8,128)(4,1)S(1)} %get-tuple-element.16, pred[24,256]{1,0:T(8,128)(4,1)S(1)} %get-tuple-element.15, pred[24,256]{1,0:T(8,128)(4,1)S(1)} %get-tuple-element.14, ...), kind=kLoop, calls=%fused_computation.2 | loop fusion | flops 2949120 | bytes 7028736 | tf_op jit(solution)/shard_map/jit(_where)/select_n | solution.py:112
  16.3 0.1 fusion.4
  16.4 0.9 copy.23
  17.3 0.0 all-gather.6.cloned.1.call-update
  17.4 0.0 all-gather.4.cloned.1.call-start
  17.4 0.9 copy.22
  18.3 0.0 all-gather.4.cloned.1.call-update
  18.4 0.0 all-gather.8.cloned.1.call-start
  18.4 0.9 copy.24
  19.3 0.0 all-gather.8.cloned.1.call-update
  20.7 0.6 gather_fusion
  21.3 0.6 gather_fusion.1
  21.9 0.7 broadcast_compare_fusion.5
  22.6 0.1 fusion.1
  22.7 0.1 fusion.5
  22.8 0.1 copy.19
  22.9 0.1 reshape.231.fock
  23.0 0.1 copy.18
  23.1 0.1 reshape.229.fock
  23.2 0.1 copy.20
  23.3 0.1 reshape.233.fock
  23.4 0.1 pad_add_fusion.scalars
  23.5 0.6 broadcast_xor_fusion
  24.1 0.6 broadcast_compare_fusion.4
  24.7 38.4 %all-gather.6.cloned.1.call-done.amps = bf16[96,10240]{1,0:T(8,128)(2,1)} async-done(((bf16[24,10240]{1,0:T(8,128)(2,1)}), bf16[96,10240]{1,0:T(8,128)(2,1)}) %all-gather.6.cloned.1.call-update) | async-done | bytes 1966096 | tf_op jit(solution)/shard_map/all_gather | solution.py:129
  63.1 1.5 copy-done
  64.7 9.7 %shard_map.65 = f32[2,96,240]{2,1,0:T(8,128)S(1)} custom-call(s32[7]{0:T(128)S(1)} %pad_add_fusion.scalars, f32[80]{0:T(128)S(1)} %reshape.231.fock, bf16[96,10240]{1,0:T(8,128)(2,1)S(1)} %copy-done, bf16[120,240,1920]{2,1,0:T(8,128)(2,1)} %refs_5_.5, bf16[120,240,1920]{2,1,0:T(8,128)(2,1)} %refs_5_.5, bf16[120,240,1920]{2,1,0:T(8,128)(2,1)} %refs_5_.5, ...), custom_call_target="tpu_custom_call" | custom-call | flops 943718400 | bytes 16711680 | tf_op jit(solution)/shard_map/pallas_call | solution.py:64
  74.4 32.8 %all-gather.4.cloned.1.call-done.amps = bf16[96,10240]{1,0:T(8,128)(2,1)} async-done(((bf16[24,10240]{1,0:T(8,128)(2,1)}), bf16[96,10240]{1,0:T(8,128)(2,1)}) %all-gather.4.cloned.1.call-update) | async-done | bytes 1966096 | tf_op jit(solution)/shard_map/all_gather | solution.py:129
  107.1 1.5 copy-done.1
  108.7 9.7 %shard_map.64 = f32[2,96,240]{2,1,0:T(8,128)S(1)} custom-call(s32[7]{0:T(128)S(1)} %pad_add_fusion.scalars, f32[80]{0:T(128)S(1)} %reshape.229.fock, bf16[96,10240]{1,0:T(8,128)(2,1)S(1)} %copy-done.1, bf16[120,240,1920]{2,1,0:T(8,128)(2,1)} %refs_5_.5, bf16[120,240,1920]{2,1,0:T(8,128)(2,1)} %refs_5_.5, bf16[120,240,1920]{2,1,0:T(8,128)(2,1)} %refs_5_.5, ...), custom_call_target="tpu_custom_call" | custom-call | flops 943718400 | bytes 16711680 | tf_op jit(solution)/shard_map/pallas_call | solution.py:64
  118.4 32.8 %all-gather.8.cloned.1.call-done.amps = bf16[96,10240]{1,0:T(8,128)(2,1)} async-done(((bf16[24,10240]{1,0:T(8,128)(2,1)}), bf16[96,10240]{1,0:T(8,128)(2,1)}) %all-gather.8.cloned.1.call-update) | async-done | bytes 1966096 | tf_op jit(solution)/shard_map/all_gather | solution.py:129
  151.2 1.5 copy-done.2
  152.7 9.5 %shard_map.66 = f32[2,96,240]{2,1,0:T(8,128)S(1)} custom-call(s32[7]{0:T(128)S(1)} %pad_add_fusion.scalars, f32[80]{0:T(128)S(1)} %reshape.233.fock, bf16[96,10240]{1,0:T(8,128)(2,1)S(1)} %copy-done.2, bf16[120,240,1920]{2,1,0:T(8,128)(2,1)} %refs_5_.5, bf16[120,240,1920]{2,1,0:T(8,128)(2,1)} %refs_5_.5, bf16[120,240,1920]{2,1,0:T(8,128)(2,1)} %refs_5_.5, ...), custom_call_target="tpu_custom_call" | custom-call | flops 943718400 | bytes 16711680 | tf_op jit(solution)/shard_map/pallas_call | solution.py:64
  162.2 0.1 select_bitcast_fusion
  162.3 0.2 copy.21
  162.5 0.2 reshape.235
  162.7 15.1 %fusion = f32[16,480]{1,0:T(8,128)S(1)} fusion(f32[96,480]{1,0:T(8,128)S(1)} %reshape.235), kind=kCustom, calls=%all-reduce-scatter | all-reduce-scatter fusion | flops 61441 | bytes 215552
  177.8 2.1 %collective-permute-start = (f32[16,480]{1,0:T(8,128)S(1)}, f32[16,480]{1,0:T(8,128)S(1)}, u32[]{:S(2)}, u32[]{:S(2)}) collective-permute-start(f32[16,480]{1,0:T(8,128)S(1)} %fusion), channel_id=1, source_target_pairs={{0,1},{1,2},{2,3},{3,4},{4,5},{5,6},{6,7},{8,9},{9,10},{10,11},{11... | collective-permute-start | bytes 92168
  179.9 4.6 %collective-permute-start.1 = (f32[12,480]{1,0:T(8,128)S(1)}, f32[12,480]{1,0:T(8,128)S(1)}, u32[]{:S(2)}, u32[]{:S(2)}) collective-permute-start(f32[12,480]{1,0:T(8,128)S(1)} %slice.56), channel_id=1, source_target_pairs={{0,2},{1,3},{2,4},{3,5},{4,6},{5,7},{8,10},{9,11},{10,12},{11,13},... | collective-permute-start | bytes 69128
  184.5 0.6 dynamic-slice.4
  185.8 0.3 concatenate.4
  186.0 0.7 reshape.236
  (30 shorter events, 0.1 us)
Async XLA Ops:
  6.5 56.6 %all-gather.6.cloned.1.call-start = ((), (), s32[]{:S(2)}) async-start(), calls=%async_computation.1 | async-start | bytes 2457600 | tf_op jit(solution)/shard_map/all_gather | solution.py:129
  8.1 0.7 copy-start.6
  8.1 4.0 %slice-start = ((bf16[24,120,960]{2,1,0:T(8,128)(2,1)}), bf16[24,120,192]{2,1,0:T(8,128)(2,1)S(1)}, s32[]{:S(2)}) async-start(bf16[24,120,960]{2,1,0:T(8,128)(2,1)} %param.6), calls=%async_computation.3 | async-start | bytes 2949120 | tf_op jit(solution)/shard_map/slice | solution.py:109
  17.4 89.8 %all-gather.4.cloned.1.call-start = ((), (), s32[]{:S(2)}) async-start(), calls=%async_computation | async-start | bytes 2457600 | tf_op jit(solution)/shard_map/all_gather | solution.py:129
  17.4 3.2 %copy-start.8 = (s32[2]{0:T(128)S(1)}, s32[2]{0:T(128)}, u32[]{:S(2)}) copy-start(s32[2]{0:T(128)} %param.11) | copy-start | bytes 28
  17.4 3.2 %copy-start.3 = (s32[960]{0:T(1024)S(1)}, s32[960]{0:T(1024)}, u32[]{:S(2)}) copy-start(s32[960]{0:T(1024)} %param.9) | copy-start | bytes 11524
  18.3 4.3 %copy-start.5 = (bf16[120,2]{0,1:T(2,128)(2,1)S(1)}, bf16[120,2]{0,1:T(2,128)(2,1)}, u32[]{:S(2)}) copy-start(bf16[120,2]{0,1:T(2,128)(2,1)} %param.8) | copy-start | bytes 1444
  18.4 132.8 %all-gather.8.cloned.1.call-start = ((), (), s32[]{:S(2)}) async-start(), calls=%async_computation.2 | async-start | bytes 2457600 | tf_op jit(solution)/shard_map/all_gather | solution.py:129
  63.1 1.5 copy-start
  107.1 1.5 copy-start.1
  151.2 1.5 copy-start.2
  152.7 9.5 %copy-start.7 = (pred[2,96]{1,0:T(4,128)(4,1)S(1)}, pred[2,96]{1,0:T(4,128)(4,1)}, u32[]{:S(2)}) copy-start(pred[2,96]{1,0:T(4,128)(4,1)} %broadcast_compare_fusion.4) | copy-start | bytes 580
  162.2 22.3 %copy-start.4 = (u32[32]{0:T(128)S(1)}, u32[32]{0:T(128)}, u32[]{:S(2)}) copy-start(u32[32]{0:T(128)} %constant.106) | copy-start | bytes 388
  177.8 8.0 %collective-permute-start = (f32[16,480]{1,0:T(8,128)S(1)}, f32[16,480]{1,0:T(8,128)S(1)}, u32[]{:S(2)}, u32[]{:S(2)}) collective-permute-start(f32[16,480]{1,0:T(8,128)S(1)} %fusion), channel_id=1, source_target_pairs={{0,1},{1,2},{2,3},{3,4},{4,5},{5,6},{6,7},{8,9},{9,10},{10,11},{11... | collective-permute-start | bytes 92168
  179.9 5.9 %collective-permute-start.1 = (f32[12,480]{1,0:T(8,128)S(1)}, f32[12,480]{1,0:T(8,128)S(1)}, u32[]{:S(2)}, u32[]{:S(2)}) collective-permute-start(f32[12,480]{1,0:T(8,128)S(1)} %slice.56), channel_id=1, source_target_pairs={{0,2},{1,3},{2,4},{3,5},{4,6},{5,7},{8,10},{9,11},{10,12},{11,13},... | collective-permute-start | bytes 69128
Sparse Core Ops, SparseCore 0:
  17.5 45.6 all-gather.5
  64.7 42.3 all-gather.3
  108.7 42.3 all-gather.7

commit v2 on v0

v2 whole, which is shorter than its diff:
```python
import functools

import jax
import jax.numpy as jnp
from jax import lax
from jax.experimental import pallas as pl
from jax.experimental.pallas import tpu as pltpu
from jax.sharding import PartitionSpec as P

LANES = 128
SPAN = 256
MESH = pl.DeviceIdType.MESH


def ladder_kernel(
    n, reps, full_virt, own, fock, orbital, panel_irreps, pair_irreps, w, out,
    amps, even, odd, acc, facc, wide, turned, terms, landed, send_sem, recv_sem, w_sem, term_send, term_recv,
):
    me = lax.axis_index("grid")
    rep = lax.axis_index("rep")
    chunks, pair_local, _ = own.shape
    depth, cols, width = even.shape
    panel = acc.shape[0]
    run = full_virt // 4
    rows = chunks * depth
    has_right, has_left = me < n - 1, me > 0
    right, left = jnp.minimum(me + 1, n - 1), jnp.maximum(me - 1, 0)

    def w_copy(chunk, slot):
        return pltpu.make_async_copy(w.at[pl.ds(chunk * depth, depth)], (even, odd)[slot], w_sem.at[slot])

    w_copy(0, 0).start()
    w_copy(1, 1).start()

    barrier = pltpu.get_barrier_semaphore()
    for there, other in ((has_right, right), (has_left, left)):
        @pl.when(there)
        def _():
            pl.semaphore_signal(barrier, inc=1, device_id={"grid": other}, device_id_type=MESH)
    for d in range(1, reps):
        pl.semaphore_signal(barrier, inc=1, device_id={"rep": lax.rem(rep + d, reps)}, device_id_type=MESH)
    pl.semaphore_wait(barrier, reps - 1 + jnp.minimum(me, 1) + jnp.minimum(n - 1 - me, 1))

    def copy(owner, chunk, way):
        return pltpu.make_async_remote_copy(
            src_ref=amps.at[owner, chunk],
            dst_ref=amps.at[owner, chunk],
            send_sem=send_sem.at[way, owner, chunk],
            recv_sem=recv_sem.at[owner, chunk],
            device_id={"grid": (right, left)[way]},
            device_id_type=MESH,
        )

    def pass_on(i):
        @pl.when(i < chunks)
        def _():
            amps[me, i] = own[i]

            @pl.when(has_right)
            def _():
                copy(me, i, 0).start()

            @pl.when(has_left)
            def _():
                copy(me, i, 1).start()

        for s in range(1, n):
            chunk = i - s
            valid = jnp.logical_and(chunk >= 0, chunk < chunks)

            @pl.when(jnp.logical_and(valid, me >= s))
            def _():
                copy(me - s, chunk, 0).wait_recv()

                @pl.when(has_right)
                def _():
                    copy(me - s, chunk, 0).start()

            @pl.when(jnp.logical_and(valid, me + s < n))
            def _():
                copy(me + s, chunk, 1).wait_recv()

                @pl.when(has_left)
                def _():
                    copy(me + s, chunk, 1).start()

    c_irrep = orbital[rep * rows]
    a_irrep = orbital[me * cols]
    panel_irrep = [panel_irreps[b] for b in range(panel)]
    starts = []
    for b in range(panel):
        wanted = c_irrep ^ a_irrep ^ panel_irrep[b]
        place = jnp.int32(0)
        for r in range(1, 4):
            place = place + jnp.where(orbital[r * run] == wanted, r, 0)
        starts.append(b * full_virt + place * run)

    acc[...] = jnp.zeros_like(acc)
    facc[...] = jnp.zeros_like(facc)
    lane = lax.broadcasted_iota(jnp.int32, (cols, LANES), 1)

    def multiply(chunk, slot):
        held = (even, odd)[slot]
        w_copy(chunk, slot).wait()
        for c in range(depth):
            at = slice(c * SPAN, (c + 1) * SPAN)
            part = jnp.concatenate([amps[s, chunk, :, at].astype(jnp.float32) for s in range(n)], axis=0)
            for b in range(panel):
                facc[b] += fock[(chunk * depth + c) * panel + b] * part
                near = pltpu.roll(part, b * full_virt % SPAN, 1) if b * full_virt % SPAN else part
                turned[b, :, at] = near.astype(jnp.bfloat16)
                for half in range(2):
                    picked = None
                    for t in range(b * full_virt // LANES, -(-(b + 1) * full_virt // LANES)):
                        if t % 2 != half:
                            continue
                        here = held[c, :, t * LANES : (t + 1) * LANES]
                        inside = jnp.logical_and(lane >= starts[b] - t * LANES, lane < starts[b] + run - t * LANES)
                        picked = here if picked is None else jnp.where(inside, here, picked)
                    wide[b, :, c * SPAN + half * LANES : c * SPAN + (half + 1) * LANES] = picked
        for b in range(panel):
            acc[b] += lax.dot_general(turned[b], wide[b], (((1,), (1,)), ((), ())), preferred_element_type=jnp.float32)

        @pl.when(chunk + 2 < chunks)
        def _():
            w_copy(chunk + 2, slot).start()

    @pl.loop(0, n - 1)
    def _(i):
        pass_on(i)

    @pl.loop(0, chunks // 2)
    def _(pair):
        for slot in range(2):
            chunk = pair * 2 + slot
            pass_on(chunk + n - 1)
            multiply(chunk, slot)

    own_shift = (n * cols * SPAN - me * cols) % SPAN
    out_rows = out.shape[1]
    for b in range(panel):
        own_cols = pltpu.roll(facc[b], own_shift, 1)[:, :cols]
        whole = acc[b] + own_cols * (panel_irrep[b] == c_irrep).astype(jnp.float32)
        whole = jnp.where(pair_irreps[...] == (panel_irrep[b] ^ a_irrep), whole, 0.0)
        for r in range(reps):
            terms[r, b] = whole[r * out_rows : (r + 1) * out_rows]

    def term_copy(d):
        peer = lax.rem(rep + d, reps)
        return pltpu.make_async_remote_copy(
            src_ref=terms.at[peer],
            dst_ref=landed.at[d],
            send_sem=term_send.at[d],
            recv_sem=term_recv.at[d],
            device_id={"rep": peer},
            device_id_type=MESH,
        )

    for d in range(1, reps):
        term_copy(d).start()
    total = terms[rep]
    for d in range(1, reps):
        term_copy(d).wait_recv()
        total = total + landed[d]
    out[...] = total
    for d in range(1, reps):
        term_copy(d).wait_send()

    @pl.loop(0, chunks)
    def _(chunk):
        for owner in range(n):
            @pl.when(jnp.logical_and(has_right, owner <= me))
            def _():
                copy(owner, chunk, 0).wait_send()

            @pl.when(jnp.logical_and(has_left, owner >= me))
            def _():
                copy(owner, chunk, 1).wait_send()


def ladder(own, fock, orbital, panel_irreps, pair_irreps, w, n, reps, full_virt):
    panel = w.shape[2] // full_virt
    rows, cols, width = w.shape
    chunks, pair_local, span = own.shape
    depth = rows // chunks
    pairs = n * pair_local
    smem = pl.BlockSpec(memory_space=pltpu.SMEM)
    vmem = pl.BlockSpec(memory_space=pltpu.VMEM)
    return pl.pallas_call(
        functools.partial(ladder_kernel, n, reps, full_virt),
        out_shape=jax.ShapeDtypeStruct((panel, pairs // reps, cols), jnp.float32),
        in_specs=[vmem, smem, smem, smem, vmem, pl.BlockSpec(memory_space=pl.ANY)],
        out_specs=vmem,
        scratch_shapes=[
            pltpu.VMEM((n, chunks, pair_local, span), jnp.bfloat16),
            pltpu.VMEM((depth, cols, width), jnp.bfloat16),
            pltpu.VMEM((depth, cols, width), jnp.bfloat16),
            pltpu.VMEM((panel, pairs, cols), jnp.float32),
            pltpu.VMEM((panel, pairs, SPAN), jnp.float32),
            pltpu.VMEM((panel, cols, span), jnp.bfloat16),
            pltpu.VMEM((panel, pairs, span), jnp.bfloat16),
            pltpu.VMEM((reps, panel, pairs // reps, cols), jnp.float32),
            pltpu.VMEM((reps, panel, pairs // reps, cols), jnp.float32),
            pltpu.SemaphoreType.DMA((2, n, chunks)),
            pltpu.SemaphoreType.DMA((n, chunks)),
            pltpu.SemaphoreType.DMA((2,)),
            pltpu.SemaphoreType.DMA((reps,)),
            pltpu.SemaphoreType.DMA((reps,)),
        ],
        compiler_params=pltpu.CompilerParams(vmem_limit_bytes=44 * 1024 * 1024, collective_id=0, has_side_effects=True),
        cost_estimate=pl.CostEstimate(
            flops=2 * pairs * rows * SPAN * cols * panel, bytes_accessed=rows * cols * width * 2, transcendentals=0
        ),
    )(own, fock, orbital, panel_irreps, pair_irreps, w)


def pick(table, index):
    found = jnp.zeros_like(index)
    for r in range(4):
        found = jnp.where(index == r, table[r], found)
    return found


def shards(amplitudes, vvvv_panel, fock_window, orbital_irrep, pair_irrep, virtual_panel):
    pair_local, virt_local, full_virt = amplitudes.shape
    run = full_virt // 4
    grid_index = lax.axis_index("grid")
    rep_index = lax.axis_index("rep")

    runs = [orbital_irrep[r * run] for r in range(4)]
    c_irrep = pick(runs, rep_index * virt_local // run)

    own_pairs = lax.dynamic_slice_in_dim(pair_irrep, grid_index * pair_local, pair_local, 0)
    wanted = own_pairs ^ c_irrep
    pair_run = sum(jnp.where(runs[r] == wanted, r, 0) for r in range(1, 4))
    span_count = -(-full_virt // SPAN)
    compact = jnp.zeros((pair_local, virt_local, SPAN), amplitudes.dtype)
    for q in range(span_count):
        width = min(SPAN, full_virt - q * SPAN)
        piece = amplitudes[:, :, q * SPAN : q * SPAN + width]
        piece = jnp.pad(piece, ((0, 0), (0, 0), (0, SPAN - width)))
        lane_run = (q * SPAN + jnp.arange(SPAN, dtype=jnp.int32)) // run
        compact = jnp.where(lane_run[None, None, :] == pair_run[:, None, None], piece, compact)

    depth = max(d for d in range(1, 9) if virt_local % (2 * d) == 0)
    chunks = virt_local // depth
    own = jnp.swapaxes(compact.reshape(pair_local, chunks, depth * SPAN), 0, 1)
    fock = fock_window.astype(jnp.float32).reshape(-1)
    sizes = lax.axis_size("grid"), lax.axis_size("rep")
    summed = ladder(own, fock, orbital_irrep, pick(runs, virtual_panel // run), pair_irrep[:, None], vvvv_panel, *sizes, full_virt)
    return jnp.swapaxes(summed, 0, 1)


def solution(mesh):
    return jax.shard_map(
        shards,
        mesh=mesh,
        in_specs=(P("grid", "rep", None), P("rep", "grid", None), P("rep", None), P(), P(), P()),
        out_specs=P("rep", None, "grid"),
        check_vma=False,
    )
```

time: 518 us -> 128 us (0.25)
  local copies, waits for them, and re-layouts: 290 us -> 5.78 us
  waiting for transfers between devices: 121 us -> 0 us
  Pallas kernels: 0 us -> 110 us
  matrix products: 56.5 us -> 0 us
  blocking collectives: 14.7 us -> 0 us
  between operations: 14.2 us -> 2.65 us
  starting transfers between devices: 6.98 us -> 0 us
    reshape x3 -> x4, local copies, waits for them, and re-layouts: 279 us -> 2 us  [the longest x2 1.75 us: shards(): own = jnp.swapaxes(compact.reshape(pair_local, chunks, depth * SPAN), 0, 1)]
    all_gather x1 -> x0, waiting for transfers between devices: 121 us -> none  [shards(): block_rows = lax.all_gather(masked_amps, 'grid', axis=0, tiled=True)]
    pallas_call x0 -> x1, Pallas kernels: none -> 110 us  [ladder(): pl.pallas_call(functools.partial(ladder_kernel, n, reps, full_virt), out_...]
    dot_general x2 -> x0, matrix products: 56.5 us -> none  [the longest x1 53.1 us: shards(): jnp.einsum('ncd,cabd->nba', block_rows, masked_w, preferred_element_type=...]
    unnamed x1 -> x0, blocking collectives: 14.7 us -> none
    dynamic_slice x4 -> x0, local copies, waits for them, and re-layouts: 8.95 us -> none  [the longest x1 6.69 us: shards(): own_cols = lax.dynamic_slice_in_dim(block_rows, col_start, col_local, 2)]
    unnamed x2 -> x0, starting transfers between devices: 6.98 us -> none
  transfers between devices with their start and end apart: 3 -> 0, of which waited for: 1 -> 0; matrix products, arithmetic and copies ran while one was open for 55% -> 0% of each run, Pallas kernels for 0% -> 0%
where the time goes in v2:
time: 128 us; the launch traced here: 127 us
  Pallas kernels  110 us (86%)
  other arithmetic  9.4 us (7%)
  local copies, waits for them, and re-layouts  5.78 us (5%)
  between operations  2.65 us (2%)
    pallas_call x1, Pallas kernels, ladder(): pl.pallas_call(functools.partial(ladder_kernel, n, reps, full_virt), out_...  110 us
    select_n x1, other arithmetic, shards(): jnp.where(lane_run[None, None, :] == pair_run[:, None, None], piece, comp...  4.15 us
    add x1, other arithmetic, shards(): pair_run = sum((jnp.where(runs[r] == wanted, r, 0) for r in range(1, 4)))  2.61 us

profile of v2, /device:TPU:1, one launch (start us, length us, event | category | flops | bytes accessed | tf_op | source)
XLA Modules:
  0.0 127.4 jit_solution(10669596445588554454)
XLA Ops:
  0.0 1.5 %fusion.2 = (s32[1]{0:T(128)}, s32[1]{0:T(128)}, s32[1]{0:T(128)}, s32[1]{0:T(128)}) fusion(s32[960]{0:T(1024)} %orbital.1), kind=kLoop, calls=%fused_computation.23 | loop fusion | bytes 32 | tf_op jit(solution)/shard_map/slice | solution.py:230
  4.0 2.6 %fusion.1 = s32[24]{0:T(128)S(1)} fusion(s32[96]{0:T(128)} %param.10, s32[]{:T(128)S(6)} %select_n.92, s32[]{:T(128)} %bitcast.1, s32[]{:T(128)} %bitcast.2, s32[]{:T(128)S(6)} %select_n.97, s32[]{:T(128)} %bitcast), kind=kLoop, calls=%fused_computation.22 | loop fusion | flops 216 | bytes 212 | tf_op jit(solution)/shard_map/add | solution.py:235
  6.7 0.1 broadcast_compare_fusion.3
  6.8 0.0 slice-start
  6.8 1.4 %slice-done = bf16[24,120,192]{2,1,0:T(8,128)(2,1)S(1)} async-done(((bf16[24,120,960]{2,1,0:T(8,128)(2,1)}), bf16[24,120,192]{2,1,0:T(8,128)(2,1)S(1)}, s32[]{:S(2)}) %slice-start) | async-done | bytes 1105944 | tf_op jit(solution)/shard_map/slice | solution.py:240
  8.1 4.2 %select_select_fusion = bf16[24,120,256]{2,1,0:T(8,128)(2,1)S(1)} fusion(bf16[24,120,960]{2,1,0:T(8,128)(2,1)} %param.6, bf16[24,120,192]{2,1,0:T(8,128)(2,1)S(1)} %slice-done, pred[24,256]{1,0:T(8,128)(4,1)S(1)} %get-tuple-element.12, pred[24,256]{1,0:T(8,128)(4,1)S(1)} %get-tuple-element.11, pred[24,256]{1,0:T(8,128)(4,1)S(1)} %get-tuple-element.10, ...), kind=kLoop, calls=%fused_computation.1 | loop fusion | flops 2949120 | bytes 7028736 | tf_op jit(solution)/shard_map/jit(_where)/select_n | solution.py:243
  12.3 1.3 %reshape.161 = bf16[24,20,1536]{2,1,0:T(8,128)(2,1)S(1)} reshape(bf16[24,120,256]{2,1,0:T(8,128)(2,1)S(1)} %select_select_fusion) | data formatting | bytes 2949120 | tf_op jit(solution)/shard_map/reshape | solution.py:247
  13.6 0.0 copy-start.3
  13.6 0.0 copy-start.2
  13.6 0.0 copy-start.1
  13.6 0.0 copy-start
  13.7 0.4 copy.14
  14.1 0.2 copy-done.3
  14.3 2.5 %compare_select_fusion.3.panel_irreps = s32[2]{0:T(128)S(1)} fusion(s32[2]{0:T(128)S(1)} %copy-done.3, s32[]{:T(128)} %bitcast.3, s32[]{:T(128)} %bitcast, s32[]{:T(128)} %bitcast.2, s32[]{:T(128)} %bitcast.1), kind=kLoop, calls=%fused_computation.12 | loop fusion | flops 32 | bytes 32 | tf_op jit(solution)/shard_map/jit(_where)/select_n | solution.py:220
  16.8 0.0 copy-done.2
  16.8 0.1 copy.10
  16.9 0.1 reshape.165.fock
  17.1 0.0 copy-done.1
  17.1 0.1 copy.11.pair_irreps
  17.2 0.0 copy-done
  17.2 109.6 %shard_map.64 = f32[2,12,240]{2,1,0:T(8,128)S(1)} custom-call(bf16[20,24,1536]{2,1,0:T(8,128)(2,1)S(1)} %bitcast.9, f32[240]{0:T(256)S(1)} %reshape.165.fock, s32[960]{0:T(1024)S(1)} %copy-done, s32[2]{0:T(128)S(1)} %compare_select_fusion.3.panel_irreps, s32[96,1]{1,0:T(8,128)S(1)} %copy.11.pair_irreps, bf16[120,240,1920]{2,1,0:T(8,128)(2,1)} %w.1), custom_call_target="tpu_custom_call" | custom-call | flops 2831155200 | bytes 110592000 | tf_op jit(solution)/shard_map/pallas_call | solution.py:189
  126.8 0.6 copy.12
  (2 shorter events, 0.0 us)
Async XLA Ops:
  6.8 1.4 %slice-start = ((bf16[24,120,960]{2,1,0:T(8,128)(2,1)}), bf16[24,120,192]{2,1,0:T(8,128)(2,1)S(1)}, s32[]{:S(2)}) async-start(bf16[24,120,960]{2,1,0:T(8,128)(2,1)} %param.6), calls=%async_computation | async-start | bytes 2949120 | tf_op jit(solution)/shard_map/slice | solution.py:240
  13.6 0.7 copy-start.3
  13.6 3.2 %copy-start.2 = (bf16[120,2]{0,1:T(2,128)(2,1)S(1)}, bf16[120,2]{0,1:T(2,128)(2,1)}, u32[]{:S(2)}) copy-start(bf16[120,2]{0,1:T(2,128)(2,1)} %param.8) | copy-start | bytes 1444
  13.6 3.4 %copy-start.1 = (s32[96]{0:T(128)S(1)}, s32[96]{0:T(128)}, u32[]{:S(2)}) copy-start(s32[96]{0:T(128)} %param.10) | copy-start | bytes 1156
  13.6 3.5 %copy-start = (s32[960]{0:T(1024)S(1)}, s32[960]{0:T(1024)}, u32[]{:S(2)}) copy-start(s32[960]{0:T(1024)} %orbital.1) | copy-start | bytes 11524
